TPU v7x, 32 devices: a whole 2x2x4 slice. The times are simulated.
32 devices in a mesh: tm: 4 (over y, x), pts: 8 (over z, core).
Axes of the slice: x: 2, y: 2, z: 4, core: 2. Of those that a mesh axis runs over, the one named last changes fastest.
Arguments:
- codes: bfloat16 [11520, 5120], P('tm', 'pts'), as said below
- scales: float32 [11520], P('tm'), may hold values from 0.005 to 0.015
- weights: float32 [5120], P('pts'), may hold values from 0.5 to 4
- freq_indices: int32 [64], replicated, may hold values from 0 to 127, as said below
Outputs:
- cross_spectral: float32 [64, 2, 89, 89], P('pts')
Inputs may be any that keep to these rules, and one draw needn't show every extreme that they name: `codes`: whole numbers. `freq_indices`: distinct bins.
All inputs are finite; a program needn't handle non-finite values.
Results may differ from a plain program's by a relative error of at most 0.0011.
Values may be sent and summed in bfloat16 or wider, within the bound.
A program may use at most 64 MiB of HBM per device.

v0:
```python
import math
import jax
import jax.numpy as jnp
from jax import lax
from jax.sharding import PartitionSpec as P

NFFT = 256


def make_tables(freq_indices):
    sample = jnp.arange(NFFT, dtype=jnp.int32)
    phases = freq_indices[:, None] * sample[None, :] % NFFT
    angles = phases.astype(jnp.float32) * (2.0 * math.pi / NFFT)
    hann_window = 0.5 - 0.5 * jnp.cos(sample.astype(jnp.float32) * (2.0 * math.pi / NFFT))
    cosine_table = (0.25 * hann_window[None, :] * jnp.cos(angles)).astype(jnp.bfloat16)
    sine_table = (-0.25 * hann_window[None, :] * jnp.sin(angles)).astype(jnp.bfloat16)
    return (cosine_table, sine_table)


def cross_matrices(stacked):
    blocks = stacked.shape[1] // 2
    products = jnp.einsum("fip,fjp->fij", stacked, stacked, preferred_element_type=jnp.float32)
    matrix_re = products[:, :blocks, :blocks] + products[:, blocks:, blocks:]
    matrix_im = products[:, :blocks, blocks:] - products[:, blocks:, :blocks]
    return jnp.stack([matrix_re, matrix_im], axis=1)


def per_device(codes, scales, weights, freq_indices):
    values = (codes.astype(jnp.float32) * scales[:, None]).astype(jnp.bfloat16)
    regrouped = lax.all_to_all(values, "tm", split_axis=1, concat_axis=0, tiled=True)
    point_count = regrouped.shape[1]
    own_weights = lax.dynamic_slice_in_dim(
        weights, lax.axis_index("tm") * point_count, point_count, 0
    )
    total_points = weights.shape[0] * lax.axis_size("pts")
    root_weight = jnp.sqrt(own_weights / total_points)
    cosine_table, sine_table = make_tables(freq_indices)
    hop_rows = regrouped.reshape(-1, NFFT // 2, point_count)
    windows = jnp.concatenate([hop_rows[:-1], hop_rows[1:]], axis=1)
    real_part = jnp.einsum("fn,bnp->fbp", cosine_table, windows, preferred_element_type=jnp.float32)
    imag_part = jnp.einsum("fn,bnp->fbp", sine_table, windows, preferred_element_type=jnp.float32)
    scaled_re = (real_part * root_weight[None, None, :]).astype(jnp.bfloat16)
    scaled_im = (imag_part * root_weight[None, None, :]).astype(jnp.bfloat16)
    stacked = jnp.concatenate([scaled_re, scaled_im], axis=1)
    partial_value = lax.psum_scatter(
        cross_matrices(stacked), "pts", scatter_dimension=0, tiled=True
    )
    return lax.psum(partial_value, "tm")


def solution(mesh):
    return jax.shard_map(
        per_device,
        mesh=mesh,
        in_specs=(P("tm", "pts"), P("tm"), P("pts"), P()),
        out_specs=P("pts", None, None, None),
        check_vma=False,
    )
```

profile of v0, /device:TPU:0, one launch (start us, length us, event | category | flops | bytes accessed | tf_op | source)
XLA Modules:
  0.0 320.9 jit_solution(16545950724297518855)
XLA Ops:
  6.5 6.2 %copy.9 = bf16[2880,640]{0,1:T(8,128)(2,1)} copy(bf16[2880,640]{1,0:T(8,128)(2,1)} %param.4) | data formatting | bytes 7372800 | tf_op args[0]
  12.7 4.6 %multiply_convert_fusion = bf16[2880,640]{0,1:T(8,128)(2,1)} fusion(bf16[2880,640]{0,1:T(8,128)(2,1)} %copy.9, f32[2880]{0:T(1024)S(1)} %copy-done), kind=kLoop, calls=%fused_computation.1 | loop fusion | flops 5529600 | bytes 7384320 | tf_op jit(solution)/shard_map/convert_element_type | solution.py:29
  17.3 5.2 %all-to-all-start = ((bf16[2880,4,160]{0,2,1:T(8,128)(2,1)}), bf16[2880,4,160]{0,2,1:T(8,128)(2,1)}, u32[]{:S(2)}, u32[]{:S(2)}) async-start(bf16[2880,4,160]{0,2,1:T(8,128)(2,1)} %bitcast.15), calls=%async_computation | async-start | bytes 7536640 | tf_op jit(solution)/shard_map/all_to_all | solution.py:30
  22.6 0.8 multiply_sqrt_fusion
  23.3 43.1 %all-to-all-done = bf16[2880,4,160]{0,2,1:T(8,128)(2,1)} async-done(((bf16[2880,4,160]{0,2,1:T(8,128)(2,1)}), bf16[2880,4,160]{0,2,1:T(8,128)(2,1)}, u32[]{:S(2)}, u32[]{:S(2)}) %all-to-all-start) | async-done | bytes 3686432 | tf_op jit(solution)/shard_map/all_to_all | solution.py:30
  66.4 5.9 %copy.10 = bf16[4,2880,160]{1,0,2:T(4,128)(2,1)} copy(bf16[4,2880,160]{1,2,0:T(8,128)(2,1)} %bitcast.2) | data formatting | bytes 7372800 | tf_op jit(solution)/shard_map/all_to_all | solution.py:30
  72.3 8.5 %reshape.24 = bf16[90,128,160]{1,0,2:T(8,128)(2,1)} reshape(bf16[4,2880,160]{1,0,2:T(4,128)(2,1)} %copy.10) | data formatting | bytes 7372800 | tf_op jit(solution)/shard_map/reshape | solution.py:38
  80.8 4.9 %fusion.32 = (bf16[89,128,160]{1,0,2:T(8,128)(2,1)S(1)}, bf16[89,128,160]{1,0,2:T(8,128)(2,1)S(1)}) fusion(bf16[90,128,160]{1,0,2:T(8,128)(2,1)} %reshape.24), kind=kLoop, calls=%fused_computation.44 | loop fusion | bytes 14581760 | tf_op jit(solution)/shard_map/slice | solution.py:39
  85.8 3.7 %multiply_convert_fusion.2 = bf16[64,89,160]{1,0,2:T(8,128)(2,1)S(1)} fusion(f32[160]{0:T(256)S(1)} %multiply_sqrt_fusion, bf16[89,128,160]{1,0,2:T(8,128)(2,1)S(1)} %get-tuple-element.8, bf16[89,128,160]{1,0,2:T(8,128)(2,1)S(1)} %get-tuple-element.7, s32[64]{0:T(128)S(1)} %copy-done.1, f32[256]{0:T(256)S(1)} %fusion.21), kind=kOutput, calls=%fused_computation.7 | convolution fusion | flops 483282944 | bytes 9115520 | tf_op jit(solution)/shard_map/fn,bnp->fbp/dot_general | solution.py:40
  89.4 3.6 %multiply_convert_fusion.1 = bf16[64,89,160]{1,0,2:T(8,128)(2,1)S(1)} fusion(f32[160]{0:T(256)S(1)} %multiply_sqrt_fusion, bf16[89,128,160]{1,0,2:T(8,128)(2,1)S(1)} %get-tuple-element.8, bf16[89,128,160]{1,0,2:T(8,128)(2,1)S(1)} %get-tuple-element.7, f32[256]{0:T(256)S(1)} %fusion.20, s32[64]{0:T(128)S(1)} %copy-done.1), kind=kOutput, calls=%fused_computation.6 | convolution fusion | flops 483282944 | bytes 9115520 | tf_op jit(solution)/shard_map/fn,bnp->fbp/dot_general | solution.py:41
  93.1 2.2 pad_maximum_fusion.2
  95.3 17.2 %fusion = f32[64,178,178]{2,1,0:T(8,128)} fusion(bf16[64,178,160]{1,0,2:T(8,128)(2,1)S(1)} %pad_maximum_fusion.2), kind=kOutput, calls=%fused_computation.4 | convolution fusion | flops 648888320 | bytes 11756544 | tf_op jit(solution)/shard_map/fip,fjp->fij/dot_general | solution.py:22
  112.5 9.8 %fusion.5 = (f32[64,1,89,89]{3,2,0,1:T(8,128)S(1)}, f32[64,1,89,89]{3,2,0,1:T(8,128)}) fusion(f32[64,178,178]{2,1,0:T(8,128)} %fusion), kind=kLoop, calls=%fused_computation.13 | loop fusion | flops 1013888 | bytes 12166656 | tf_op jit(solution)/shard_map/stack | solution.py:25
  122.3 2.6 pad_maximum_fusion.1
  124.9 7.8 %copy.13 = f32[64,2,89,89]{3,1,2,0:T(2,128)} copy(f32[64,2,89,89]{3,2,0,1:T(8,128)S(1)} %pad_maximum_fusion.1) | data formatting | bytes 8111104 | tf_op jit(solution)/shard_map/stack | solution.py:25
  132.7 0.0 all-reduce.6.cloned.1.call-update
  132.7 0.0 all-reduce.4.cloned.1.call-start
  132.8 0.6 copy-done.2
  133.4 0.6 dynamic-slice
  134.6 126.2 %all-reduce.6.cloned.1.call-done = f32[64,2,89,89]{3,1,2,0:T(2,128)} async-done(((f32[64,2,89,89]{3,1,2,0:T(2,128)}), f32[64,2,89,89]{3,1,2,0:T(2,128)}) %all-reduce.6.cloned.1.call-update) | async-done | bytes 4055568
  260.8 2.0 constant_dynamic-slice_fusion
  262.8 0.0 all-reduce.4.cloned.1.call-update
  262.8 49.2 %all-reduce.4.cloned.1.call-done = f32[8,2,89,89]{3,1,2,0:T(2,128)} async-done(((f32[8,2,89,89]{3,1,2,0:T(2,128)}), f32[8,2,89,89]{3,1,2,0:T(2,128)}) %all-reduce.4.cloned.1.call-update) | async-done | bytes 506960 | tf_op jit(solution)/shard_map/psum | solution.py:48
  312.0 2.0 copy.18
  (8 shorter events, 0.1 us)
Async XLA Ops:
  6.5 6.2 %copy-start = (f32[2880]{0:T(1024)S(1)}, f32[2880]{0:T(1024)}, u32[]{:S(2)}) copy-start(f32[2880]{0:T(1024)} %param.5) | copy-start | bytes 34564
  17.3 49.1 %all-to-all-start = ((bf16[2880,4,160]{0,2,1:T(8,128)(2,1)}), bf16[2880,4,160]{0,2,1:T(8,128)(2,1)}, u32[]{:S(2)}, u32[]{:S(2)}) async-start(bf16[2880,4,160]{0,2,1:T(8,128)(2,1)} %bitcast.15), calls=%async_computation | async-start | bytes 7536640 | tf_op jit(solution)/shard_map/all_to_all | solution.py:30
  22.5 238.3 %all-reduce.6.cloned.1.call-start = ((), (), s32[]{:S(2)}) async-start(), calls=%async_computation.2 | async-start | bytes 11665408
  80.8 4.9 %copy-start.1 = (s32[64]{0:T(128)S(1)}, s32[64]{0:T(128)}, u32[]{:S(2)}) copy-start(s32[64]{0:T(128)} %param.7) | copy-start | bytes 772
  132.7 0.7 copy-start.2
  132.7 179.3 %all-reduce.4.cloned.1.call-start = ((), (), s32[]{:S(2)}) async-start(), calls=%async_computation.1 | async-start | bytes 1458176 | tf_op jit(solution)/shard_map/psum | solution.py:48
Sparse Core Ops, SparseCore 0:
  132.9 127.8 all-reduce.5
  263.9 48.1 all-reduce.3
where the time goes:
time: 322 us; the launch traced here: 321 us
  waiting for transfers between devices  219 us (68%)
  local copies, waits for them, and re-layouts  38.5 us (12%)
  matrix products  24.5 us (8%)
  other arithmetic  20.1 us (6%)
  between operations  14.1 us (4%)
  starting transfers between devices  5.21 us (2%)
    unnamed x3, waiting for transfers between devices  126 us
    psum x1, waiting for transfers between devices, per_device(): return lax.psum(partial_value, 'tm')  49.2 us
    all_to_all x1, waiting for transfers between devices, per_device(): lax.all_to_all(values, 'tm', split_axis=1, concat_axis=0, tiled=True)  43.1 us
    dot_general x1, matrix products, cross_matrices(): jnp.einsum('fip,fjp->fij', stacked, stacked, preferred_element_type=jnp.f...  17.2 us
    another operation x2, other arithmetic, cross_matrices(): return jnp.stack([matrix_re, matrix_im], axis=1)  12.4 us
    unnamed x10, local copies, waits for them, and re-layouts  11.4 us
    reshape x1, local copies, waits for them, and re-layouts, per_device(): hop_rows = regrouped.reshape(-1, NFFT // 2, point_count)  8.52 us
    another operation x1, local copies, waits for them, and re-layouts, cross_matrices(): return jnp.stack([matrix_re, matrix_im], axis=1)  7.81 us
  transfers between devices with their start and end apart: 3, of which 3 were waited for; matrix products, arithmetic and copies ran while one was open for 0% of the time, Pallas kernels for 0%

commit v1 on v0

--- a/solution.py
+++ b/solution.py
@@ -27,7 +27,19 @@
 
 def per_device(codes, scales, weights, freq_indices):
     values = (codes.astype(jnp.float32) * scales[:, None]).astype(jnp.bfloat16)
-    regrouped = lax.all_to_all(values, "tm", split_axis=1, concat_axis=0, tiled=True)
+    ways, here = (lax.axis_size("tm"), lax.axis_index("tm"))
+    width = values.shape[1] // ways
+    shape = list(values.shape)
+    shape[1] = width
+    height = shape[0]
+    shape[0] = height * ways
+    full = jnp.zeros(shape, values.dtype)
+    for mask in range(ways):
+        part = lax.dynamic_slice_in_dim(values, (here ^ mask) * width, width, axis=1)
+        if mask:
+            part = lax.ppermute(part, "tm", [(d, d ^ mask) for d in range(ways)])
+        full = lax.dynamic_update_slice_in_dim(full, part, (here ^ mask) * height, axis=0)
+    regrouped = full
     point_count = regrouped.shape[1]
     own_weights = lax.dynamic_slice_in_dim(
         weights, lax.axis_index("tm") * point_count, point_count, 0

time: 322 us -> 350 us (1.087)
  local copies, waits for them, and re-layouts: 38.5 us -> 89.8 us
  waiting for transfers between devices: 219 us -> 195 us
    all_to_all x1 -> x0, waiting for transfers between devices: 43.1 us -> none  [per_device(): lax.all_to_all(values, 'tm', split_axis=1, concat_axis=0, tiled=True)]
    dynamic_update_slice x0 -> x4, local copies, waits for them, and re-layouts: none -> 37.3 us  [per_device(): lax.dynamic_update_slice_in_dim(full, part, (here ^ mask) * height, axis=0)]
    ppermute x0 -> x3, waiting for transfers between devices: none -> 19.1 us  [per_device(): part = lax.ppermute(part, 'tm', [(d, d ^ mask) for d in range(ways)])]
    slice x1 -> x3, local copies, waits for them, and re-layouts: 4.92 us -> 20.2 us  [per_device(): windows = jnp.concatenate([hop_rows[:-1], hop_rows[1:]], axis=1)]
    reshape x1 -> x0, local copies, waits for them, and re-layouts: 8.52 us -> none  [per_device(): hop_rows = regrouped.reshape(-1, NFFT // 2, point_count)]
    all_to_all x1 -> x0, local copies, waits for them, and re-layouts: 5.86 us -> none  [per_device(): lax.all_to_all(values, 'tm', split_axis=1, concat_axis=0, tiled=True)]
    all_to_all x1 -> x0, starting transfers between devices: 5.16 us -> none  [per_device(): lax.all_to_all(values, 'tm', split_axis=1, concat_axis=0, tiled=True)]
    unnamed x10 -> x13, local copies, waits for them, and re-layouts: 11.4 us -> 16.2 us
  transfers between devices with their start and end apart: 3 -> 5, of which waited for: 3 -> 4; matrix products, arithmetic and copies ran while one was open for 0% -> 9% of each run, Pallas kernels for 0% -> 0%
where the time goes in v1:
time: 350 us; the launch traced here: 349 us
  waiting for transfers between devices  195 us (56%)
  local copies, waits for them, and re-layouts  89.8 us (26%)
  matrix products  26.9 us (8%)
  other arithmetic  18.2 us (5%)
  between operations  14.1 us (4%)
  starting transfers between devices  4.5 us (1%)
    unnamed x3, waiting for transfers between devices  127 us
    psum x1, waiting for transfers between devices, per_device(): return lax.psum(partial_value, 'tm')  49.2 us
    dynamic_update_slice x4, local copies, waits for them, and re-layouts, per_device(): lax.dynamic_update_slice_in_dim(full, part, (here ^ mask) * height, axis=0)  37.3 us
    slice x3, local copies, waits for them, and re-layouts, per_device(): windows = jnp.concatenate([hop_rows[:-1], hop_rows[1:]], axis=1)  20.2 us
    ppermute x3, waiting for transfers between devices, per_device(): part = lax.ppermute(part, 'tm', [(d, d ^ mask) for d in range(ways)])  19.1 us
    dot_general x1, matrix products, cross_matrices(): jnp.einsum('fip,fjp->fij', stacked, stacked, preferred_element_type=jnp.f...  17.1 us
    unnamed x13, local copies, waits for them, and re-layouts  16.2 us
    another operation x2, other arithmetic, cross_matrices(): return jnp.stack([matrix_re, matrix_im], axis=1)  12.4 us
  transfers between devices with their start and end apart: 5, of which 4 were waited for; matrix products, arithmetic and copies ran while one was open for 9% of the time, Pallas kernels for 0%

profile of v1, /device:TPU:0, one launch (start us, length us, event | category | flops | bytes accessed | tf_op | source)
XLA Modules:
  0.0 348.6 jit_solution(1986767015137077375)
XLA Ops:
  6.5 6.2 %copy.8 = bf16[2880,640]{0,1:T(8,128)(2,1)} copy(bf16[2880,640]{1,0:T(8,128)(2,1)} %param.4) | data formatting | bytes 7372800 | tf_op args[0]
  12.7 2.7 multiply_convert_fusion
  17.1 2.9 collective-permute-start
  21.5 2.0 broadcast_in_dim.2
  23.6 8.9 %dynamic_update_slice.12 = bf16[11520,160]{0,1:T(8,128)(2,1)} dynamic-update-slice(bf16[11520,160]{0,1:T(8,128)(2,1)} %broadcast_in_dim.2, bf16[2880,160]{0,1:T(8,128)(2,1)S(1)} %get-tuple-element.10, s32[]{:T(128)S(6)} %select_n.34, s32[]{:T(128)} %constant.20.clone.1) | dynamic-update-slice | bytes 1843204 | tf_op jit(solution)/shard_map/dynamic_update_slice | solution.py:41
  33.4 8.6 %collective-permute-done = bf16[2880,160]{0,1:T(8,128)(2,1)} collective-permute-done((bf16[2880,160]{0,1:T(8,128)(2,1)}, bf16[2880,160]{0,1:T(8,128)(2,1)}, u32[]{:S(2)}, u32[]{:S(2)}) %collective-permute-start) | collective-permute-done | bytes 921632 | tf_op jit(solution)/shard_map/ppermute | solution.py:40
  42.0 10.3 %dynamic_update_slice.13 = bf16[11520,160]{0,1:T(8,128)(2,1)} dynamic-update-slice(bf16[11520,160]{0,1:T(8,128)(2,1)} %dynamic_update_slice.12, bf16[2880,160]{0,1:T(8,128)(2,1)} %collective-permute-done, s32[]{:T(128)S(6)} %select_n.36, s32[]{:T(128)} %constant.20.clone.1) | dynamic-update-slice | bytes 1843204 | tf_op jit(solution)/shard_map/dynamic_update_slice | solution.py:41
  52.3 10.5 %collective-permute-done.1 = bf16[2880,160]{0,1:T(8,128)(2,1)S(1)} collective-permute-done((bf16[2880,160]{0,1:T(8,128)(2,1)}, bf16[2880,160]{0,1:T(8,128)(2,1)S(1)}, u32[]{:S(2)}, u32[]{:S(2)}) %collective-permute-start.1) | collective-permute-done | bytes 921632 | tf_op jit(solution)/shard_map/ppermute | solution.py:40
  62.7 8.9 %dynamic_update_slice.14 = bf16[11520,160]{0,1:T(8,128)(2,1)} dynamic-update-slice(bf16[11520,160]{0,1:T(8,128)(2,1)} %dynamic_update_slice.13, bf16[2880,160]{0,1:T(8,128)(2,1)S(1)} %collective-permute-done.1, s32[]{:T(128)S(6)} %select_n.38, s32[]{:T(128)} %constant.20.clone.1) | dynamic-update-slice | bytes 1843204 | tf_op jit(solution)/shard_map/dynamic_update_slice | solution.py:41
  71.6 9.2 %dynamic_update_slice.15 = bf16[11520,160]{0,1:T(8,128)(2,1)} dynamic-update-slice(bf16[11520,160]{0,1:T(8,128)(2,1)} %dynamic_update_slice.14, bf16[2880,160]{0,1:T(8,128)(2,1)S(1)} %collective-permute-done.2, s32[]{:T(128)S(6)} %select_n.40, s32[]{:T(128)} %constant.20.clone.1) | dynamic-update-slice | bytes 1843204 | tf_op jit(solution)/shard_map/dynamic_update_slice | solution.py:41
  80.8 6.5 %fusion.28 = (bf16[11392,160]{0,1:T(8,128)(2,1)}, bf16[11392,160]{0,1:T(8,128)(2,1)}) fusion(bf16[11520,160]{0,1:T(8,128)(2,1)} %dynamic_update_slice.15), kind=kLoop, calls=%fused_computation.45 | loop fusion | bytes 14581760 | tf_op jit(solution)/shard_map/slice | solution.py:51
  87.3 6.8 %slice.25 = bf16[89,128,160]{1,0,2:T(8,128)(2,1)} reshape(bf16[11392,160]{0,1:T(8,128)(2,1)} %get-tuple-element.12) | data formatting | bytes 7290880 | tf_op jit(solution)/shard_map/slice | solution.py:51
  94.2 4.8 %constant_dynamic-update-slice_fusion.1 = bf16[89,256,160]{1,0,2:T(8,128)(2,1)} fusion(bf16[89,128,160]{1,0,2:T(8,128)(2,1)} %slice.25), kind=kLoop, calls=%fused_computation.27 | loop fusion | bytes 7577600
  99.0 6.8 %slice.27 = bf16[89,128,160]{1,0,2:T(8,128)(2,1)} reshape(bf16[11392,160]{0,1:T(8,128)(2,1)} %get-tuple-element.11) | data formatting | bytes 7290880 | tf_op jit(solution)/shard_map/slice | solution.py:51
  105.8 4.7 %constant_dynamic-update-slice_fusion = bf16[89,256,160]{1,0,2:T(8,128)(2,1)} fusion(bf16[89,256,160]{1,0,2:T(8,128)(2,1)} %constant_dynamic-update-slice_fusion.1, bf16[89,128,160]{1,0,2:T(8,128)(2,1)} %slice.27), kind=kLoop, calls=%fused_computation.26 | loop fusion | bytes 7864320 | tf_op jit(solution)/shard_map/concatenate | solution.py:51
  110.5 6.5 %multiply_convert_fusion.2 = bf16[64,89,160]{1,0,2:T(8,128)(2,1)S(1)} fusion(f32[160]{0:T(256)S(1)} %multiply_sqrt_fusion, bf16[89,256,160]{1,0,2:T(8,128)(2,1)} %constant_dynamic-update-slice_fusion, s32[64]{0:T(128)S(1)} %copy-done.2, f32[256]{0:T(256)S(1)} %fusion.21), kind=kOutput, calls=%fused_computation.6 | convolution fusion | flops 468701184 | bytes 9115520 | tf_op jit(solution)/shard_map/fn,bnp->fbp/dot_general | solution.py:52
  117.1 3.2 multiply_convert_fusion.1
  120.3 2.2 pad_maximum_fusion.1
  122.5 17.1 %fusion = f32[64,178,178]{2,1,0:T(8,128)} fusion(bf16[64,178,160]{1,0,2:T(8,128)(2,1)S(1)} %pad_maximum_fusion.1), kind=kOutput, calls=%fused_computation.3 | convolution fusion | flops 648888320 | bytes 11756544 | tf_op jit(solution)/shard_map/fip,fjp->fij/dot_general | solution.py:22
  139.6 9.8 %fusion.3 = (f32[64,1,89,89]{3,2,0,1:T(8,128)S(1)}, f32[64,1,89,89]{3,2,0,1:T(8,128)}) fusion(f32[64,178,178]{2,1,0:T(8,128)} %fusion), kind=kLoop, calls=%fused_computation.10 | loop fusion | flops 1013888 | bytes 12166656 | tf_op jit(solution)/shard_map/stack | solution.py:25
  149.5 2.6 pad_maximum_fusion
  152.1 7.8 %copy.11 = f32[64,2,89,89]{3,1,2,0:T(2,128)} copy(f32[64,2,89,89]{3,2,0,1:T(8,128)S(1)} %pad_maximum_fusion) | data formatting | bytes 8111104 | tf_op jit(solution)/shard_map/stack | solution.py:25
  161.8 126.7 %all-reduce.6.cloned.1.call-done = f32[64,2,89,89]{3,1,2,0:T(2,128)} async-done(((f32[64,2,89,89]{3,1,2,0:T(2,128)}), f32[64,2,89,89]{3,1,2,0:T(2,128)}) %all-reduce.6.cloned.1.call-update) | async-done | bytes 4055568
  290.6 49.2 %all-reduce.4.cloned.1.call-done = f32[8,2,89,89]{3,1,2,0:T(2,128)} async-done(((f32[8,2,89,89]{3,1,2,0:T(2,128)}), f32[8,2,89,89]{3,1,2,0:T(2,128)}) %all-reduce.4.cloned.1.call-update) | async-done | bytes 506960 | tf_op jit(solution)/shard_map/psum | solution.py:60
  (22 shorter events, 9.3 us)
Async XLA Ops:
  6.5 6.2 %copy-start.1 = (f32[2880]{0:T(1024)S(1)}, f32[2880]{0:T(1024)}, u32[]{:S(2)}) copy-start(f32[2880]{0:T(1024)} %param.5) | copy-start | bytes 34564
  6.5 282.0 %all-reduce.6.cloned.1.call-start = ((), (), s32[]{:S(2)}) async-start(), calls=%async_computation.1 | async-start | bytes 11665408
  17.1 25.0 %collective-permute-start = (bf16[2880,160]{0,1:T(8,128)(2,1)}, bf16[2880,160]{0,1:T(8,128)(2,1)}, u32[]{:S(2)}, u32[]{:S(2)}) collective-permute-start(bf16[2880,160]{0,1:T(8,128)(2,1)} %get-tuple-element.9), channel_id=1, source_target_pairs={{0,8},{8,0},{16,24},{24,16},{1,9},{9,1},{17,25},{25,17},{2,10},{10... | collective-permute-start | bytes 2764808 | tf_op jit(solution)/shard_map/ppermute | solution.py:40
  20.0 42.7 %collective-permute-start.1 = (bf16[2880,160]{0,1:T(8,128)(2,1)}, bf16[2880,160]{0,1:T(8,128)(2,1)S(1)}, u32[]{:S(2)}, u32[]{:S(2)}) collective-permute-start(bf16[2880,160]{0,1:T(8,128)(2,1)} %get-tuple-element.8), channel_id=1, source_target_pairs={{0,16},{8,24},{16,0},{24,8},{1,17},{9,25},{17,1},{25,9},{2,18},{10... | collective-permute-start | bytes 2764808 | tf_op jit(solution)/shard_map/ppermute | solution.py:40
  21.5 50.1 %collective-permute-start.2 = (bf16[2880,160]{0,1:T(8,128)(2,1)}, bf16[2880,160]{0,1:T(8,128)(2,1)S(1)}, u32[]{:S(2)}, u32[]{:S(2)}) collective-permute-start(bf16[2880,160]{0,1:T(8,128)(2,1)} %get-tuple-element.7), channel_id=1, source_target_pairs={{0,24},{8,16},{16,8},{24,0},{1,25},{9,17},{17,9},{25,1},{2,26},{10... | collective-permute-start | bytes 2764808 | tf_op jit(solution)/shard_map/ppermute | solution.py:40
  105.8 4.7 %copy-start.2 = (s32[64]{0:T(128)S(1)}, s32[64]{0:T(128)}, u32[]{:S(2)}) copy-start(s32[64]{0:T(128)} %param.7) | copy-start | bytes 772
  110.5 6.6 %copy-start = (bf16[89,256,160]{1,0,2:T(8,128)(2,1)S(1)}, bf16[89,256,160]{1,0,2:T(8,128)(2,1)}, u32[]{:S(2)}) copy-start(bf16[89,256,160]{1,0,2:T(8,128)(2,1)} %constant_dynamic-update-slice_fusion) | copy-start | bytes 21872644
  159.9 0.7 copy-start.3
  159.9 179.8 %all-reduce.4.cloned.1.call-start = ((), (), s32[]{:S(2)}) async-start(), calls=%async_computation | async-start | bytes 1458176 | tf_op jit(solution)/shard_map/psum | solution.py:60
Sparse Core Ops, SparseCore 0:
  160.0 128.4 all-reduce.5
  291.6 48.1 all-reduce.3
